TPU v7x, 32 devices: a whole 2x2x4 slice. The times are simulated.
32 devices in a mesh: groups: 2 (over y), dp: 4 (over z), tensor: 2 (over x), seq: 2 (over core).
Axes of the slice: x: 2, y: 2, z: 4, core: 2. Of those that a mesh axis runs over, the one named last changes fastest.
Arguments:
- pas_q: bfloat16 [32, 256, 1024], P(('groups', 'dp', 'seq'), None, 'tensor'), parts along dimension 0, may hold values from -12 to 12
- pas_kv: bfloat16 [2, 32, 256, 256], P(None, ('groups', 'dp', 'seq'), None, 'tensor'), parts along dimension 1, may hold values from -6 to 6
- pre_kv: bfloat16 [2, 8, 256, 256], P(None, ('groups', 'dp'), 'seq', 'tensor'), parts along dimension 1, may hold values from -8 to 8
- d_out: bfloat16 [32, 256, 1024], P(('groups', 'dp', 'seq'), None, 'tensor'), parts along dimension 0, may hold values from -24 to 24
- passage_query: int32 [32], P('groups'), parts along dimension 0, may hold values from 0 to 3, never falling along the last dimension, each value on 1 to 8 neighbouring positions
- query_owner: int32 [8], P('groups'), parts along dimension 0, may hold values from 0 to 3, each once
Outputs:
- attn_out: bfloat16 [32, 256, 1024], P(('groups', 'dp', 'seq'), None, 'tensor'), parts along dimension 0
- d_q: bfloat16 [32, 256, 1024], P(('groups', 'dp', 'seq'), None, 'tensor'), parts along dimension 0
- d_pas_kv: bfloat16 [2, 32, 256, 256], P(None, ('groups', 'dp', 'seq'), None, 'tensor'), parts along dimension 1
- d_pre_kv: bfloat16 [2, 8, 256, 256], P(None, ('groups', 'dp'), 'seq', 'tensor'), parts along dimension 1
There are 2 independent parts, one for each index of `groups`. A program takes and returns all parts, laid end to end along the dimension named above; each array names one. Nothing has to cross between parts.
Inputs may be any that keep to these rules, and one draw needn't show every extreme that they name: `passage_query`: passages are packed by query: the candidates of one query are consecutive passages; every query has 1 to 8 candidates and one query has exactly 8. `query_owner`: each slot holds the prefix of exactly one query.
All inputs are finite; a program needn't handle non-finite values.
Results may differ from a plain program's by a relative error of at most 0.02.
Values may be sent and summed in bfloat16 or wider, within the bound.
A program may use at most 64 MiB of HBM per device.

v0:
```python
import jax
import jax.numpy as jnp
from jax import lax
from jax.sharding import PartitionSpec as P

HD = 128
GROUP = 4


def attend_passage(position, pas_q, pas_kv, d_out, lookup, prefix_all):
    query_rows = lax.dynamic_index_in_dim(pas_q, position, 0, False)
    token_count = query_rows.shape[0]
    queries = query_rows.reshape(token_count, GROUP, HD)
    grad_rows = lax.dynamic_index_in_dim(d_out, position, 0, False).reshape(token_count, GROUP, HD)
    own_kv = lax.dynamic_index_in_dim(pas_kv, position, 1, False)
    slot_id = lax.dynamic_index_in_dim(lookup, position, 0, False)
    prefix = lax.dynamic_index_in_dim(prefix_all, slot_id, 1, False)
    prefix_len = prefix.shape[1]
    key_rows = jnp.concatenate([prefix[0], own_kv[0]], axis=0)
    value_rows = jnp.concatenate([prefix[1], own_kv[1]], axis=0)
    scaling = HD ** (-0.5)
    scores = (
        jnp.einsum("thd,kd->thk", queries, key_rows, preferred_element_type=jnp.float32) * scaling
    )
    token_pos = jnp.arange(token_count)[:, None]
    column = jnp.arange(key_rows.shape[0])[None, :]
    visible = column - prefix_len <= token_pos
    scores = jnp.where(visible[:, None, :], scores, -jnp.inf)
    row_top = jnp.max(scores, axis=-1, keepdims=True)
    log_total = row_top + jnp.log(jnp.sum(jnp.exp(scores - row_top), axis=-1, keepdims=True))
    weights = jnp.exp(scores - log_total)
    weight_round = weights.astype(jnp.bfloat16)
    out_round = jnp.einsum(
        "thk,kd->thd", weight_round, value_rows, preferred_element_type=jnp.float32
    ).astype(jnp.bfloat16)
    row_delta = jnp.sum(
        grad_rows.astype(jnp.float32) * out_round.astype(jnp.float32), axis=-1, keepdims=True
    )
    prob_grad = jnp.einsum("thd,kd->thk", grad_rows, value_rows, preferred_element_type=jnp.float32)
    score_grad = (weights * (prob_grad - row_delta)).astype(jnp.bfloat16)
    query_grad = (
        jnp.einsum("thk,kd->thd", score_grad, key_rows, preferred_element_type=jnp.float32)
        * scaling
    ).astype(jnp.bfloat16)
    key_grad = (
        jnp.einsum("thk,thd->kd", score_grad, queries, preferred_element_type=jnp.float32) * scaling
    )
    value_grad = jnp.einsum(
        "thk,thd->kd", weight_round, grad_rows, preferred_element_type=jnp.float32
    )
    return (
        out_round.reshape(token_count, GROUP * HD),
        query_grad.reshape(token_count, GROUP * HD),
        key_grad,
        value_grad,
    )


def on_device(pas_q, pas_kv, pre_kv, d_out, passage_query, query_owner):
    local_count = pas_q.shape[0]
    dp_count = lax.axis_size("dp")
    seq_count = lax.axis_size("seq")
    dp_index = lax.axis_index("dp")
    first_row = (dp_index * seq_count + lax.axis_index("seq")) * local_count
    local_query = lax.dynamic_slice_in_dim(passage_query, first_row, local_count)
    query_total = query_owner.shape[0]
    matches = local_query[:, None] == jnp.arange(query_total, dtype=jnp.int32)[None, :]
    slot_ids = jnp.sum(jnp.where(matches, query_owner[None, :], 0), axis=1)
    joined = lax.all_gather(pre_kv, "seq", axis=2, tiled=True)
    prefix_all = lax.all_gather(joined, "dp", axis=1, tiled=True)
    prefix_len = prefix_all.shape[2]

    def per_passage(position):
        return attend_passage(position, pas_q, pas_kv, d_out, slot_ids, prefix_all)

    attn_out, d_q, key_grads, value_grads = lax.map(
        per_passage, jnp.arange(local_count, dtype=jnp.int32)
    )
    d_pas_kv = jnp.stack([key_grads[:, prefix_len:], value_grads[:, prefix_len:]]).astype(
        jnp.bfloat16
    )
    prefix_terms = jnp.stack([key_grads[:, :prefix_len], value_grads[:, :prefix_len]], axis=1)
    slot_count = pre_kv.shape[1]
    part_len = pre_kv.shape[2]
    selector = (
        slot_ids[:, None] == jnp.arange(dp_count * slot_count, dtype=jnp.int32)[None, :]
    ).astype(jnp.float32)
    split_terms = prefix_terms.reshape(local_count, 2, seq_count, part_len, HD)
    partial_value = jnp.einsum(
        "pab,pxshd->xasbhd",
        selector.reshape(local_count, dp_count, slot_count),
        split_terms,
        precision=lax.Precision.HIGHEST,
    )
    partial_value = partial_value.astype(jnp.bfloat16).reshape(
        2, dp_count * seq_count * slot_count, part_len, HD
    )
    summed = lax.psum_scatter(partial_value, ("dp", "seq"), scatter_dimension=1, tiled=True).astype(
        jnp.float32
    )
    d_pre_kv = summed.astype(jnp.bfloat16)
    return (attn_out, d_q, d_pas_kv, d_pre_kv)


def solution(mesh):
    return jax.shard_map(
        on_device,
        mesh=mesh,
        in_specs=(
            P(("groups", "dp", "seq"), None, "tensor"),
            P(None, ("groups", "dp", "seq"), None, "tensor"),
            P(None, ("groups", "dp"), "seq", "tensor"),
            P(("groups", "dp", "seq"), None, "tensor"),
            P("groups"),
            P("groups"),
        ),
        out_specs=(
            P(("groups", "dp", "seq"), None, "tensor"),
            P(("groups", "dp", "seq"), None, "tensor"),
            P(None, ("groups", "dp", "seq"), None, "tensor"),
            P(None, ("groups", "dp"), "seq", "tensor"),
        ),
        check_vma=False,
    )
```

profile of v0, /device:TPU:0, one launch (start us, length us, event | category | flops | bytes accessed | tf_op | source)
XLA Modules:
  0.0 130.8 jit_solution(15183227288582284619)
XLA Ops:
  7.2 0.0 all-reduce.3.cloned.1.call-start
  7.3 2.4 %all_gather.6 = bf16[2,1,256,128]{3,2,1,0:T(8,128)(2,1)S(1)} all-gather(bf16[2,1,128,128]{3,2,1,0:T(8,128)(2,1)} %param.10), channel_id=1, replica_groups=mesh['groups'=2,'dp'=4,'tensor'=2,'seq'=2] {'seq'}, dimensions={2}, use_global_device_ids=true | all-gather | bytes 196608 | tf_op jit(solution)/shard_map/all_gather | solution.py:69
  9.6 17.9 %all_gather.7 = bf16[2,4,256,128]{3,2,1,0:T(8,128)(2,1)} all-gather(bf16[2,1,256,128]{3,2,1,0:T(8,128)(2,1)S(1)} %all_gather.6), channel_id=1, replica_groups=mesh['groups'=2,'dp'=4,'tensor'=2,'seq'=2] {'dp'}, dimensions={1}, use_global_device_ids=true | all-gather | bytes 655360 | tf_op jit(solution)/shard_map/all_gather | solution.py:70
  27.6 0.7 dynamic_slice.44
  28.3 0.8 fusion.20
  29.1 30.0 %while.18 = (s32[]{:T(128)}, bf16[2,256,512]{2,1,0:T(8,128)(2,1)}, bf16[2,256,512]{2,1,0:T(8,128)(2,1)}, f32[2,512,128]{2,1,0:T(8,128)}, f32[2,512,128]{2,1,0:T(...) while((s32[]{:T(128)}, bf16[2,256,512]{2,1,0:T(8,128)(2,1)}, ...), condition=%wide.region_5.6_spmd, body=%wide.region_1.5_spmd.sunk | while | flops 814283264 | bytes 29933972 | solution.py:76
  29.1 0.6 dynamic_slice.51
  31.7 0.6 dynamic_slice.52
  34.2 0.1 iota_compare_fusion.2
  34.3 1.0 dynamic-slice_bitcast_fusion.5
  35.3 1.1 constant_dynamic-slice_fusion.4
  36.3 0.1 copy.89
  36.5 0.1 copy.90
  36.6 0.6 fusion.49
  37.2 0.6 exponential_reduce_fusion.2
  37.9 0.7 multiply_reduce_fusion.2
  38.6 0.1 copy.91
  38.7 0.7 constant_dynamic-update-slice_fusion.4
  39.4 1.5 %fusion.52 = f32[2,512,128]{2,1,0:T(8,128)} fusion(f32[2,512,128]{2,1,0:T(8,128)} %get-tuple-element.351, s32[]{:T(128)S(6)} %copy.102, bf16[256,4,128]{0,2,1:T(8,128)(2,1)S(1)} %bitcast.115, f32[256,4,512]{2,0,1:T(8,128)S(1)} %get-tuple-element.327, f32[256,4]{0,1:T(4,128)S(1)} %log_add_fusion.2), kind=kOutput, calls=%fused_computation.9.clone.1 | convolution fusion | flops 135266304 | bytes 2625540 | tf_op jit(solution)/shard_map/while/body/eval_jaxpr/thk,thd->kd/dot_general | solution.py:48
  40.9 0.6 multiply_convert_fusion.2
  41.5 0.0 copy-start.2
  41.5 0.5 fusion.50
  42.0 0.0 copy-done
  42.0 0.5 fusion.51
  42.5 0.0 copy-start.1
  42.5 0.1 copy.92
  42.7 0.0 copy-done.2
  42.7 0.6 copy-done.1
  43.4 0.8 copy-done.3
  44.1 0.6 dynamic_slice.51
  46.7 0.6 dynamic_slice.52
  49.2 0.1 iota_compare_fusion.2
  49.3 1.0 dynamic-slice_bitcast_fusion.5
  50.3 1.1 constant_dynamic-slice_fusion.4
  51.3 0.1 copy.89
  51.5 0.1 copy.90
  51.6 0.6 fusion.49
  52.2 0.6 exponential_reduce_fusion.2
  52.9 0.7 multiply_reduce_fusion.2
  53.6 0.1 copy.91
  53.7 0.7 constant_dynamic-update-slice_fusion.4
  54.4 1.5 %fusion.52 = f32[2,512,128]{2,1,0:T(8,128)} fusion(f32[2,512,128]{2,1,0:T(8,128)} %get-tuple-element.351, s32[]{:T(128)S(6)} %copy.102, bf16[256,4,128]{0,2,1:T(8,128)(2,1)S(1)} %bitcast.115, f32[256,4,512]{2,0,1:T(8,128)S(1)} %get-tuple-element.327, f32[256,4]{0,1:T(4,128)S(1)} %log_add_fusion.2), kind=kOutput, calls=%fused_computation.9.clone.1 | convolution fusion | flops 135266304 | bytes 2625540 | tf_op jit(solution)/shard_map/while/body/eval_jaxpr/thk,thd->kd/dot_general | solution.py:48
  55.9 0.6 multiply_convert_fusion.2
  56.5 0.0 copy-start.2
  56.5 0.5 fusion.50
  57.0 0.0 copy-done
  57.0 0.5 fusion.51
  57.5 0.0 copy-start.1
  57.5 0.1 copy.92
  57.7 0.6 copy-done.1
  58.4 0.8 copy-done.3
  59.1 1.0 slice.45
  60.1 1.0 slice.44
  61.1 0.0 copy-start.4
  61.1 0.2 copy.61
  61.3 0.2 copy.62
  61.5 1.3 fusion.12
  62.8 0.9 copy.63
  63.8 0.0 all-reduce.3.cloned.1.call-update
  63.8 0.6 dynamic-slice
  64.4 1.1 fusion.16
  65.5 0.7 pad_maximum_fusion
  66.2 55.7 %all-reduce.3.cloned.1.call-done = bf16[2,8,128,128]{3,2,1,0:T(8,128)(2,1)} async-done(((bf16[2,8,128,128]{3,2,1,0:T(8,128)(2,1)}), bf16[2,8,128,128]{3,2,1,0:T(8,128)(2,1)}) %all-reduce.3.cloned.1.call-update) | async-done | bytes 524304
  121.9 2.1 %constant_dynamic-slice_fusion.2 = bf16[2,1,128,128]{3,2,1,0:T(8,128)(2,1)} fusion(bf16[2,8,128,128]{3,2,1,0:T(8,128)(2,1)} %all-reduce.3.cloned.1.call-done, u32[]{:T(128)} %bitcast.35), kind=kLoop, calls=%fused_computation.47 | loop fusion | bytes 131076
  (17 shorter events, 0.1 us)
Async XLA Ops:
  7.2 114.7 %all-reduce.3.cloned.1.call-start = ((), (), s32[]{:S(2)}) async-start(), calls=%async_computation | async-start | bytes 1048576
  40.9 1.1 copy-start
  41.5 1.2 copy-start.2
  42.5 0.8 copy-start.1
  43.3 0.8 copy-start.3
  55.9 1.1 copy-start
  56.5 1.2 copy-start.2
  57.5 0.8 copy-start.1
  58.4 0.8 copy-start.3
  61.1 2.7 %copy-start.4 = (u32[32]{0:T(128)S(1)}, u32[32]{0:T(128)}, u32[]{:S(2)}) copy-start(u32[32]{0:T(128)} %constant.93) | copy-start | bytes 388
Sparse Core Ops, SparseCore 0:
  63.9 57.9 all-reduce.2
where the time goes:
time: 131 us
  waiting for transfers between devices  55.7 us (43%)
  blocking collectives  20.3 us (15%)
  local copies, waits for them, and re-layouts  19.6 us (15%)
  between operations  14.1 us (11%)
  matrix products  9.98 us (8%)
  loops' own time  8.04 us (6%)
  other arithmetic  3.04 us (2%)
    unnamed x2, waiting for transfers between devices  55.7 us
    all_gather x1, blocking collectives, on_device(): prefix_all = lax.all_gather(joined, 'dp', axis=1, tiled=True)  17.9 us
    another operation x1, loops' own time, on_device(): lax.map(per_passage, jnp.arange(local_count, dtype=jnp.int32))  8.04 us
    dot_general x2, matrix products, attend_passage(): jnp.einsum('thk,thd->kd', weight_round, grad_rows, preferred_element_type...  2.92 us
    while x16, local copies, waits for them, and re-layouts  2.83 us
    unnamed x4, local copies, waits for them, and re-layouts  2.69 us
  transfers between devices with their start and end apart: 1, of which 1 were waited for; matrix products, arithmetic and copies ran while one was open for 2% of the time, Pallas kernels for 0%

commit v1 on v0

v1 whole, which is shorter than its diff:
```python
import math

import jax
import jax.numpy as jnp
from jax import lax
from jax.experimental import pallas as pl
from jax.experimental.pallas import tpu as pltpu
from jax.sharding import PartitionSpec as P

HD = 128
SCALE = HD ** (-0.5)
EXP_SCALE = SCALE * math.log2(math.e)
MASKED = -1e30
BF = jnp.bfloat16
F32 = jnp.float32


def dot(a, b):
    return jnp.dot(a, b, preferred_element_type=F32)


def make_kernel(n, count, heads, tokens, part):
    prefix = 2 * part

    def kernel(
        pq_ref, qo_ref, q_hbm, kv_hbm, pre_hbm, do_hbm,
        out_hbm, dq_hbm, dkv_hbm, dpre_hbm,
        q, do, kv, q_t, do_t, kv_t, e_own, dp_own, o_own, ds_pre, o_t, stat,
        pre, kv_pre, kv_pre_t, grad, own_grad, out, dq, dkv, dpre,
        send1, recv1, send2, recv2,
        load_sem, store_sem, own_sem,
        zs_sem, zr_sem, fs_sem, fr_sem, s1_sem, r1_sem, s2_sem, r2_sem,
    ):
        z = lax.axis_index("dp")
        c = lax.axis_index("seq")
        other = 1 - c

        loads = [
            pltpu.make_async_copy(q_hbm, q, load_sem.at[0]),
            pltpu.make_async_copy(kv_hbm, kv, load_sem.at[1]),
            pltpu.make_async_copy(do_hbm, do, load_sem.at[2]),
        ]
        for copy in loads:
            copy.start()
        own = pltpu.make_async_copy(pre_hbm.at[:, 0], pre.at[z, :, c], own_sem)
        own.start()

        barrier = pltpu.get_barrier_semaphore()
        for d in range(1, n):
            pl.semaphore_signal(barrier, inc=1, device_id={"dp": lax.rem(z + d, n)})
        pl.semaphore_signal(barrier, inc=1, device_id={"seq": other})
        pl.semaphore_wait(barrier, n)

        gathers = {}
        for d in range(1, n):
            gathers[d] = pltpu.make_async_remote_copy(
                src_ref=pre_hbm.at[:, 0], dst_ref=pre.at[z, :, c],
                send_sem=zs_sem.at[d], recv_sem=zr_sem.at[d],
                device_id={"dp": lax.rem(z + d, n)},
            )
            gathers[d].start()
        forwards = {}
        forwards[0] = pltpu.make_async_remote_copy(
            src_ref=pre_hbm.at[:, 0], dst_ref=pre.at[z, :, c],
            send_sem=fs_sem.at[0], recv_sem=fr_sem.at[0], device_id={"seq": other},
        )
        forwards[0].start()
        for copy in loads:
            copy.wait()

        for p in range(count):
            kv_t[0, p] = kv[0, p].T
            kv_t[1, p] = kv[1, p].T
        key_at = lax.broadcasted_iota(jnp.int32, (tokens, tokens), 0)
        token_at = lax.broadcasted_iota(jnp.int32, (tokens, tokens), 1)

        def own_part(h, _):
            cols = pl.ds(pl.multiple_of(h * HD, HD), HD)
            for p in range(count):
                qt = q[p, :, cols].T
                dt = do[p, :, cols].T
                q_t[p, h] = qt
                do_t[p, h] = dt
                scores = jnp.where(key_at <= token_at, dot(kv[0, p], qt), MASKED)
                top = jnp.max(scores, axis=0, keepdims=True)
                e = jnp.exp2((scores - top) * EXP_SCALE)
                stat[p, h, 0:1, :] = top
                stat[p, h, 1:2, :] = jnp.sum(e, axis=0, keepdims=True)
                e_own[p, h] = e
                o_own[p, h] = dot(kv_t[1, p], e.astype(BF))
                dp_own[p, h] = dot(kv[1, p], dt)
            return 0

        lax.fori_loop(0, heads, own_part, 0)

        own.wait()
        for d in range(1, n):
            gathers[d].wait_recv()
            source = lax.rem(z + n - d, n)
            forwards[d] = pltpu.make_async_remote_copy(
                src_ref=pre.at[source, :, c], dst_ref=pre.at[source, :, c],
                send_sem=fs_sem.at[d], recv_sem=fr_sem.at[d], device_id={"seq": other},
            )
            forwards[d].start()
        for d in range(n):
            forwards[d].wait_recv()

        first = (z * 2 + c) * count
        slots = [qo_ref[pq_ref[first + p]] for p in range(count)]
        for p in range(count):
            for x in range(2):
                rows = pre[slots[p], x].reshape(prefix, HD)
                kv_pre[x, p] = rows
                kv_pre_t[x, p] = rows.T
        grad[...] = jnp.zeros_like(grad)

        def prefix_part(h, _):
            cols = pl.ds(pl.multiple_of(h * HD, HD), HD)
            for p in range(count):
                dt = do_t[p, h]
                scores = dot(kv_pre[0, p], q_t[p, h])
                top_own = stat[p, h, 0:1, :]
                top = jnp.maximum(top_own, jnp.max(scores, axis=0, keepdims=True))
                shrink = jnp.exp2((top_own - top) * EXP_SCALE)
                e = jnp.exp2((scores - top) * EXP_SCALE)
                total = stat[p, h, 1:2, :] * shrink + jnp.sum(e, axis=0, keepdims=True)
                inverse = 1.0 / total
                w = e * inverse
                wb = w.astype(BF)
                factor = shrink * inverse
                o = (o_own[p, h] * factor + dot(kv_pre_t[1, p], wb)).astype(BF)
                o_t[p, h] = o
                delta = jnp.sum(dt.astype(F32) * o.astype(F32), axis=0, keepdims=True)
                stat[p, h, 2:3, :] = factor
                stat[p, h, 3:4, :] = delta
                ds = (w * (dot(kv_pre[1, p], dt) - delta)).astype(BF)
                ds_pre[p, h] = ds
                grad[p, 0] += dot(ds, q[p, :, cols])
                grad[p, 1] += dot(wb, do[p, :, cols])
            return 0

        lax.fori_loop(0, heads, prefix_part, 0)

        def half_terms(d, half):
            slot = lax.rem(z + d, n)
            rows = pl.ds(pl.multiple_of(half * part, part), part)
            values = []
            for x in range(2):
                value = None
                for p in range(count):
                    use = jnp.where(slots[p] == slot, SCALE if x == 0 else 1.0, 0.0).astype(F32)
                    term = grad[p, x, rows, :] * use
                    value = term if value is None else value + term
                values.append(value)
            return values

        order = list(range(1, n)) + [0]
        pairs = {}
        for d in order:
            values = half_terms(d, other)
            for x in range(2):
                send1[d, x] = values[x].astype(BF)
            pairs[d] = pltpu.make_async_remote_copy(
                src_ref=send1.at[d], dst_ref=recv1.at[d],
                send_sem=s1_sem.at[d], recv_sem=r1_sem.at[d], device_id={"seq": other},
            )
            pairs[d].start()

        for p in range(count):
            for h in range(heads):
                out[p, :, h * HD:(h + 1) * HD] = o_t[p, h].T
        store_out = pltpu.make_async_copy(out, out_hbm, store_sem.at[0])
        store_out.start()

        spreads = {}
        for d in range(1, n):
            values = half_terms(d, c)
            pairs[d].wait_recv()
            for x in range(2):
                send2[d, x] = (values[x] + recv1[d, x].astype(F32)).astype(BF)
            spreads[d] = pltpu.make_async_remote_copy(
                src_ref=send2.at[d], dst_ref=recv2.at[d],
                send_sem=s2_sem.at[d], recv_sem=r2_sem.at[d],
                device_id={"dp": lax.rem(z + d, n)},
            )
            spreads[d].start()

        def rest_part(h, carry):
            cols = pl.ds(pl.multiple_of(h * HD, HD), HD)
            for p in range(count):
                w = e_own[p, h] * stat[p, h, 2:3, :]
                ds = (w * (dp_own[p, h] - stat[p, h, 3:4, :])).astype(BF)
                own_grad[p, 0] += dot(ds, q[p, :, cols])
                own_grad[p, 1] += dot(w.astype(BF), do[p, :, cols])
                back = dot(kv_t[0, p], ds) + dot(kv_pre_t[0, p], ds_pre[p, h])
                dq[p, :, cols] = (back * SCALE).astype(BF).T
            return carry

        own_grad[...] = jnp.zeros_like(own_grad)
        lax.fori_loop(0, heads, rest_part, 0)
        store_dq = pltpu.make_async_copy(dq, dq_hbm, store_sem.at[1])
        store_dq.start()
        for p in range(count):
            dkv[0, p] = (own_grad[p, 0] * SCALE).astype(BF)
            dkv[1, p] = own_grad[p, 1].astype(BF)
        store_dkv = pltpu.make_async_copy(dkv, dkv_hbm, store_sem.at[2])
        store_dkv.start()

        values = half_terms(0, c)
        pairs[0].wait_recv()
        totals = [values[x] + recv1[0, x].astype(F32) for x in range(2)]
        for d in range(1, n):
            spreads[d].wait_recv()
            for x in range(2):
                totals[x] = totals[x] + recv2[d, x].astype(F32)
        for x in range(2):
            dpre[x, 0] = totals[x].astype(BF)
        store_dpre = pltpu.make_async_copy(dpre, dpre_hbm, store_sem.at[3])
        store_dpre.start()

        for d in range(1, n):
            gathers[d].wait_send()
            spreads[d].wait_send()
        for d in range(n):
            forwards[d].wait_send()
            pairs[d].wait_send()
        store_out.wait()
        store_dq.wait()
        store_dkv.wait()
        store_dpre.wait()

    return kernel


def on_device(n, pas_q, pas_kv, pre_kv, d_out, passage_query, query_owner):
    count, tokens, width = pas_q.shape
    heads = width // HD
    part = pre_kv.shape[2]
    prefix = 2 * part
    assert pre_kv.shape[1] == 1
    block = (2, part, HD)
    any_spec = pl.BlockSpec(memory_space=pl.ANY)
    smem_spec = pl.BlockSpec(memory_space=pltpu.SMEM)
    square = (count, heads, tokens, tokens)
    dma = pltpu.SemaphoreType.DMA
    call = pl.pallas_call(
        make_kernel(n, count, heads, tokens, part),
        out_shape=(
            jax.ShapeDtypeStruct(pas_q.shape, BF),
            jax.ShapeDtypeStruct(pas_q.shape, BF),
            jax.ShapeDtypeStruct(pas_kv.shape, BF),
            jax.ShapeDtypeStruct(pre_kv.shape, BF),
        ),
        in_specs=[smem_spec, smem_spec, any_spec, any_spec, any_spec, any_spec],
        out_specs=(any_spec,) * 4,
        scratch_shapes=[
            pltpu.VMEM(pas_q.shape, BF),
            pltpu.VMEM(pas_q.shape, BF),
            pltpu.VMEM(pas_kv.shape, BF),
            pltpu.VMEM((count, heads, HD, tokens), BF),
            pltpu.VMEM((count, heads, HD, tokens), BF),
            pltpu.VMEM((2, count, HD, tokens), BF),
            pltpu.VMEM(square, F32),
            pltpu.VMEM(square, F32),
            pltpu.VMEM((count, heads, HD, tokens), F32),
            pltpu.VMEM((count, heads, prefix, tokens), BF),
            pltpu.VMEM((count, heads, HD, tokens), BF),
            pltpu.VMEM((count, heads, 8, tokens), F32),
            pltpu.VMEM((n, 2, 2, part, HD), BF),
            pltpu.VMEM((2, count, prefix, HD), BF),
            pltpu.VMEM((2, count, HD, prefix), BF),
            pltpu.VMEM((count, 2, prefix, HD), F32),
            pltpu.VMEM((count, 2, tokens, HD), F32),
            pltpu.VMEM(pas_q.shape, BF),
            pltpu.VMEM(pas_q.shape, BF),
            pltpu.VMEM(pas_kv.shape, BF),
            pltpu.VMEM(pre_kv.shape, BF),
            pltpu.VMEM((n,) + block, BF),
            pltpu.VMEM((n,) + block, BF),
            pltpu.VMEM((n,) + block, BF),
            pltpu.VMEM((n,) + block, BF),
            dma((3,)),
            dma((4,)),
            dma,
        ] + [dma((n,))] * 8,
        compiler_params=pltpu.CompilerParams(
            collective_id=0, has_side_effects=True, vmem_limit_bytes=40 * 1024 * 1024
        ),
    )
    return call(passage_query, query_owner, pas_q, pas_kv, pre_kv, d_out)


def solution(mesh):
    n = mesh.shape["dp"]

    def step(*arrays):
        return on_device(n, *arrays)

    return jax.shard_map(
        step,
        mesh=mesh,
        in_specs=(
            P(("groups", "dp", "seq"), None, "tensor"),
            P(None, ("groups", "dp", "seq"), None, "tensor"),
            P(None, ("groups", "dp"), "seq", "tensor"),
            P(("groups", "dp", "seq"), None, "tensor"),
            P("groups"),
            P("groups"),
        ),
        out_specs=(
            P(("groups", "dp", "seq"), None, "tensor"),
            P(("groups", "dp", "seq"), None, "tensor"),
            P(None, ("groups", "dp", "seq"), None, "tensor"),
            P(None, ("groups", "dp"), "seq", "tensor"),
        ),
        check_vma=False,
    )
```

time: 131 us -> 34.3 us (0.26)
  waiting for transfers between devices: 55.7 us -> 0 us
  Pallas kernels: 0 us -> 25.2 us
  blocking collectives: 20.3 us -> 0 us
  between operations: 14.1 us -> 0.66 us
  local copies, waits for them, and re-layouts: 19.6 us -> 8.09 us
  matrix products: 9.98 us -> 0 us
  loops' own time: 8.04 us -> 0 us
  other arithmetic: 3.04 us -> 0 us
    unnamed x2 -> x0, waiting for transfers between devices: 55.7 us -> none
    pallas_call x0 -> x1, Pallas kernels: none -> 25.2 us  [on_device(): return call(passage_query, query_owner, pas_q, pas_kv, pre_kv, d_out)]
    all_gather x2 -> x0, blocking collectives: 20.3 us -> none  [the longest x1 17.9 us: on_device(): prefix_all = lax.all_gather(joined, 'dp', axis=1, tiled=True)]
    dot_general x13 -> x0, matrix products: 9.98 us -> none  [the longest x2 2.92 us: attend_passage(): jnp.einsum('thk,thd->kd', weight_round, grad_rows, preferred_element_type...]
    another operation x1 -> x0, loops' own time: 8.04 us -> none  [on_device(): lax.map(per_passage, jnp.arange(local_count, dtype=jnp.int32))]
    dynamic_slice x11 -> x0, local copies, waits for them, and re-layouts: 5.74 us -> none  [the longest x4 2.41 us: attend_passage(): lax.dynamic_index_in_dim(d_out, position, 0, False)]
    unnamed x4 -> x16, local copies, waits for them, and re-layouts: 2.69 us -> 8.09 us
    while x16 -> x0, local copies, waits for them, and re-layouts: 2.83 us -> none
  transfers between devices with their start and end apart: 1 -> 0, of which waited for: 1 -> 0; matrix products, arithmetic and copies ran while one was open for 2% -> 0% of each run, Pallas kernels for 0% -> 0%
where the time goes in v1:
time: 34.3 us; the launch traced here: 34 us
  Pallas kernels  25.2 us (73%)
  local copies, waits for them, and re-layouts  8.09 us (24%)
  between operations  0.66 us (2%)
    pallas_call x1, Pallas kernels, on_device(): return call(passage_query, query_owner, pas_q, pas_kv, pre_kv, d_out)  25.2 us
    unnamed x16, local copies, waits for them, and re-layouts  8.09 us

profile of v1, /device:TPU:0, one launch (start us, length us, event | category | flops | bytes accessed | tf_op | source)
XLA Modules:
  0.0 34.0 jit_solution(18435389631838220374)
XLA Ops:
  0.6 0.0 copy-start
  0.6 1.0 %copy-done = bf16[2,256,512]{2,1,0:T(8,128)(2,1)S(1)} copy-done((bf16[2,256,512]{2,1,0:T(8,128)(2,1)S(1)}, bf16[2,256,512]{2,1,0:T(8,128)(2,1)}, u32[]{:S(2)}) %copy-start) | copy-done | bytes 524312
  1.7 0.0 copy-start.1
  1.7 1.0 %copy-done.1 = bf16[2,256,512]{2,1,0:T(8,128)(2,1)S(1)} copy-done((bf16[2,256,512]{2,1,0:T(8,128)(2,1)S(1)}, bf16[2,256,512]{2,1,0:T(8,128)(2,1)}, u32[]{:S(2)}) %copy-start.1) | copy-done | bytes 524312
  2.7 0.0 copy-start.2
  2.7 0.9 %copy-done.2 = bf16[2,2,256,128]{3,2,1,0:T(8,128)(2,1)S(1)} copy-done((bf16[2,2,256,128]{3,2,1,0:T(8,128)(2,1)S(1)}, bf16[2,2,256,128]{3,2,1,0:T(8,128)(2,1)}, u32[]{:S(2)}) %copy-start.2) | copy-done | bytes 262168
  3.7 0.0 copy-start.3
  3.7 0.8 %copy-done.3 = bf16[2,1,128,128]{3,2,1,0:T(8,128)(2,1)S(1)} copy-done((bf16[2,1,128,128]{3,2,1,0:T(8,128)(2,1)S(1)}, bf16[2,1,128,128]{3,2,1,0:T(8,128)(2,1)}, u32[]{:S(2)}) %copy-start.3) | copy-done | bytes 65560
  4.5 0.0 copy-start.4
  4.5 0.7 %copy-done.4 = s32[16]{0:T(128)S(1)} copy-done((s32[16]{0:T(128)S(1)}, s32[16]{0:T(128)}, u32[]{:S(2)}) %copy-start.4) | copy-done | bytes 88
  5.2 0.0 copy-start.5
  5.2 0.7 %copy-done.5 = s32[4]{0:T(128)S(1)} copy-done((s32[4]{0:T(128)S(1)}, s32[4]{0:T(128)}, u32[]{:S(2)}) %copy-start.5) | copy-done | bytes 40
  5.8 25.2 %shard_map.93 = (bf16[2,256,512]{2,1,0:T(8,128)(2,1)S(1)}, bf16[2,256,512]{2,1,0:T(8,128)(2,1)S(1)}, bf16[2,2,256,128]{3,2,1,0:T(8,128)(2,1)S(1)}, bf16[2,1,128,128]{3,2,1,0:T(8,128)(2,1)S(1)}) custom-call(s32[16]{0:T(128)S(1)} %copy-done.4, s32[4]{0:T(128)S(1)} %copy-done.5, bf16[2,256,512]{2,1,0:T(8,128)(2,1)S(1)} %copy-done, ...), custom_call_target="tpu_custom_call" | custom-call | tf_op jit(solution)/shard_map/pallas_call | solution.py:290
  31.1 0.8 %copy.14 = bf16[2,256,512]{2,1,0:T(8,128)(2,1)} copy(bf16[2,256,512]{2,1,0:T(8,128)(2,1)S(1)} %get-tuple-element.8) | data formatting | bytes 1048576
  31.9 0.8 %copy.15 = bf16[2,256,512]{2,1,0:T(8,128)(2,1)} copy(bf16[2,256,512]{2,1,0:T(8,128)(2,1)S(1)} %get-tuple-element.9) | data formatting | bytes 1048576
  32.7 0.7 %copy.16 = bf16[2,2,256,128]{3,2,1,0:T(8,128)(2,1)} copy(bf16[2,2,256,128]{3,2,1,0:T(8,128)(2,1)S(1)} %get-tuple-element.10) | data formatting | bytes 524288
  33.4 0.6 %copy.17 = bf16[2,1,128,128]{3,2,1,0:T(8,128)(2,1)} copy(bf16[2,1,128,128]{3,2,1,0:T(8,128)(2,1)S(1)} %get-tuple-element.11) | data formatting | bytes 131072
Async XLA Ops:
  0.6 1.0 %copy-start = (bf16[2,256,512]{2,1,0:T(8,128)(2,1)S(1)}, bf16[2,256,512]{2,1,0:T(8,128)(2,1)}, u32[]{:S(2)}) copy-start(bf16[2,256,512]{2,1,0:T(8,128)(2,1)} %q_hbm.1) | copy-start | bytes 1572868
  1.7 1.0 %copy-start.1 = (bf16[2,256,512]{2,1,0:T(8,128)(2,1)S(1)}, bf16[2,256,512]{2,1,0:T(8,128)(2,1)}, u32[]{:S(2)}) copy-start(bf16[2,256,512]{2,1,0:T(8,128)(2,1)} %do_hbm.1) | copy-start | bytes 1572868
  2.7 0.9 %copy-start.2 = (bf16[2,2,256,128]{3,2,1,0:T(8,128)(2,1)S(1)}, bf16[2,2,256,128]{3,2,1,0:T(8,128)(2,1)}, u32[]{:S(2)}) copy-start(bf16[2,2,256,128]{3,2,1,0:T(8,128)(2,1)} %kv_hbm.1) | copy-start | bytes 786436
  3.7 0.8 %copy-start.3 = (bf16[2,1,128,128]{3,2,1,0:T(8,128)(2,1)S(1)}, bf16[2,1,128,128]{3,2,1,0:T(8,128)(2,1)}, u32[]{:S(2)}) copy-start(bf16[2,1,128,128]{3,2,1,0:T(8,128)(2,1)} %pre_hbm.1) | copy-start | bytes 196612
  4.5 0.7 %copy-start.4 = (s32[16]{0:T(128)S(1)}, s32[16]{0:T(128)}, u32[]{:S(2)}) copy-start(s32[16]{0:T(128)} %pq_ref.1) | copy-start | bytes 196
  5.2 0.7 %copy-start.5 = (s32[4]{0:T(128)S(1)}, s32[4]{0:T(128)}, u32[]{:S(2)}) copy-start(s32[4]{0:T(128)} %qo_ref.1) | copy-start | bytes 52

commit v2 on v1

--- a/solution.py
+++ b/solution.py
@@ -23,12 +23,12 @@
     prefix = 2 * part
 
     def kernel(
-        pq_ref, qo_ref, q_hbm, kv_hbm, pre_hbm, do_hbm,
+        pq_hbm, qo_hbm, q_hbm, kv_hbm, pre_hbm, do_hbm,
         out_hbm, dq_hbm, dkv_hbm, dpre_hbm,
         q, do, kv, q_t, do_t, kv_t, e_own, dp_own, o_own, ds_pre, o_t, stat,
         pre, kv_pre, kv_pre_t, grad, own_grad, out, dq, dkv, dpre,
         send1, recv1, send2, recv2,
-        load_sem, store_sem, own_sem,
+        pq_ref, qo_ref, load_sem, store_sem, own_sem,
         zs_sem, zr_sem, fs_sem, fr_sem, s1_sem, r1_sem, s2_sem, r2_sem,
     ):
         z = lax.axis_index("dp")
@@ -39,6 +39,8 @@
             pltpu.make_async_copy(q_hbm, q, load_sem.at[0]),
             pltpu.make_async_copy(kv_hbm, kv, load_sem.at[1]),
             pltpu.make_async_copy(do_hbm, do, load_sem.at[2]),
+            pltpu.make_async_copy(pq_hbm, pq_ref, load_sem.at[3]),
+            pltpu.make_async_copy(qo_hbm, qo_ref, load_sem.at[4]),
         ]
         for copy in loads:
             copy.start()
@@ -231,6 +233,28 @@
 
     return kernel
 
+def store_kernel(*refs):
+    sems = refs[-1]
+    count = (len(refs) - 1) // 2
+    copies = [
+        pltpu.make_async_copy(refs[i], refs[count + i], sems.at[i]) for i in range(count)
+    ]
+    for copy in copies:
+        copy.start()
+    for copy in copies:
+        copy.wait()
+
+
+def store_all(arrays):
+    any_spec = pl.BlockSpec(memory_space=pl.ANY)
+    return pl.pallas_call(
+        store_kernel,
+        out_shape=tuple(jax.ShapeDtypeStruct(a.shape, a.dtype) for a in arrays),
+        in_specs=[any_spec] * len(arrays),
+        out_specs=(any_spec,) * len(arrays),
+        scratch_shapes=[pltpu.SemaphoreType.DMA((len(arrays),))],
+    )(*(pltpu.with_memory_space_constraint(a, pltpu.VMEM) for a in arrays))
+
 
 def on_device(n, pas_q, pas_kv, pre_kv, d_out, passage_query, query_owner):
     count, tokens, width = pas_q.shape
@@ -239,8 +263,7 @@
     prefix = 2 * part
     assert pre_kv.shape[1] == 1
     block = (2, part, HD)
-    any_spec = pl.BlockSpec(memory_space=pl.ANY)
-    smem_spec = pl.BlockSpec(memory_space=pltpu.SMEM)
+    any_spec = pl.BlockSpec(memory_space=pltpu.HBM)
     square = (count, heads, tokens, tokens)
     dma = pltpu.SemaphoreType.DMA
     call = pl.pallas_call(
@@ -251,7 +274,7 @@
             jax.ShapeDtypeStruct(pas_kv.shape, BF),
             jax.ShapeDtypeStruct(pre_kv.shape, BF),
         ),
-        in_specs=[smem_spec, smem_spec, any_spec, any_spec, any_spec, any_spec],
+        in_specs=[any_spec] * 6,
         out_specs=(any_spec,) * 4,
         scratch_shapes=[
             pltpu.VMEM(pas_q.shape, BF),
@@ -279,7 +302,9 @@
             pltpu.VMEM((n,) + block, BF),
             pltpu.VMEM((n,) + block, BF),
             pltpu.VMEM((n,) + block, BF),
-            dma((3,)),
+            pltpu.SMEM(passage_query.shape, jnp.int32),
+            pltpu.SMEM(query_owner.shape, jnp.int32),
+            dma((5,)),
             dma((4,)),
             dma,
         ] + [dma((n,))] * 8,
@@ -287,7 +312,8 @@
             collective_id=0, has_side_effects=True, vmem_limit_bytes=40 * 1024 * 1024
         ),
     )
-    return call(passage_query, query_owner, pas_q, pas_kv, pre_kv, d_out)
+    arrays = (passage_query, query_owner, pas_q, pas_kv, pre_kv, d_out)
+    return store_all(call(*(pltpu.with_memory_space_constraint(a, pltpu.HBM) for a in arrays)))
 
 
 def solution(mesh):

time: 34.3 us -> 26.7 us (0.78)
  local copies, waits for them, and re-layouts: 8.09 us -> 0 us
  Pallas kernels: 25.2 us -> 25.9 us
    unnamed x16 -> x0, local copies, waits for them, and re-layouts: 8.09 us -> none
    pallas_call x1 -> x2, Pallas kernels: 25.2 us -> 25.9 us  [the longest x1 24.8 us: on_device(): call(*(pltpu.with_memory_space_constraint(a, pltpu.HBM) for a in arrays))]
where the time goes in v2:
time: 26.7 us; the launch traced here: 26.6 us
  Pallas kernels  25.9 us (97%)
  between operations  0.64 us (2%)
    pallas_call x1, Pallas kernels, on_device(): call(*(pltpu.with_memory_space_constraint(a, pltpu.HBM) for a in arrays))  24.8 us
    pallas_call x1, Pallas kernels, store_all(): pl.pallas_call(store_kernel, out_shape=tuple((jax.ShapeDtypeStruct(a.shap...  1.1 us

profile of v2, /device:TPU:0, one launch (start us, length us, event | category | flops | bytes accessed | tf_op | source)
XLA Modules:
  0.0 26.6 jit_solution(15809505844161730298)
XLA Ops:
  0.6 24.8 %shard_map.93 = (bf16[2,256,512]{2,1,0:T(8,128)(2,1)S(1)}, bf16[2,256,512]{2,1,0:T(8,128)(2,1)S(1)}, bf16[2,2,256,128]{3,2,1,0:T(8,128)(2,1)S(1)}, bf16[2,1,128,128]{3,2,1,0:T(8,128)(2,1)S(1)}) custom-call(s32[16]{0:T(128)} %pq_hbm.1, s32[4]{0:T(128)} %qo_hbm.1, bf16[2,256,512]{2,1,0:T(8,128)(2,1)} %q_hbm.1, bf16[2,2,256,128]{3,2,1,0:T(8,128)(2,1)} %kv_hbm.1, ...), custom_call_target="tpu_custom_call" | custom-call | tf_op jit(solution)/shard_map/pallas_call | solution.py:316
  25.5 1.1 %shard_map.94 = (bf16[2,256,512]{2,1,0:T(8,128)(2,1)}, bf16[2,256,512]{2,1,0:T(8,128)(2,1)}, bf16[2,2,256,128]{3,2,1,0:T(8,128)(2,1)}, bf16[2,1,128,128]{3,2,1,0:T(8,128)(2,1)}) custom-call(bf16[2,256,512]{2,1,0:T(8,128)(2,1)S(1)} %get-tuple-element.8.refs_0_, bf16[2,256,512]{2,1,0:T(8,128)(2,1)S(1)} %get-tuple-element.9.refs_1_, ...), custom_call_target="tpu_custom_call" | custom-call | tf_op jit(solution)/shard_map/pallas_call | solution.py:250

commit v3 on v2

v3 whole, which is shorter than its diff:
```python
import math

import jax
import jax.numpy as jnp
from jax import lax
from jax.experimental import pallas as pl
from jax.experimental.pallas import tpu as pltpu
from jax.sharding import PartitionSpec as P

HD = 128
SCALE = HD ** (-0.5)
EXP_SCALE = SCALE * math.log2(math.e)
MASKED = -1e30
BF = jnp.bfloat16
F32 = jnp.float32
UNROLL = 4


def dot(a, b):
    return jnp.dot(a, b, preferred_element_type=F32)


def make_kernel(n, count, heads, tokens, part):
    prefix = 2 * part

    def kernel(
        pq_hbm, qo_hbm, q_hbm, kv_hbm, pre_hbm, do_hbm,
        out_hbm, dq_hbm, dkv_hbm, dpre_hbm,
        q, do, kv, q_t, do_t, kv_t, e_own, dp_own, o_own, ds_pre, o_t, stat,
        pre_k, pre_v, kv_pre, kv_pre_t, grad, own_grad, w_pre, out, dq, dkv, dpre,
        send1, recv1, send2, recv2,
        pq_ref, qo_ref, load_sem, store_sem, own_sem,
        zs_sem, zr_sem, fs_sem, fr_sem, s1_sem, r1_sem, s2_sem, r2_sem,
    ):
        z = lax.axis_index("dp")
        c = lax.axis_index("seq")
        other = 1 - c

        barrier = pltpu.get_barrier_semaphore()
        for d in range(1, n):
            pl.semaphore_signal(barrier, inc=1, device_id={"dp": lax.rem(z + d, n)})
        pl.semaphore_signal(barrier, inc=1, device_id={"seq": other})

        pre = (pre_k, pre_v)
        own = [
            pltpu.make_async_copy(pre_hbm.at[x, 0], pre[x].at[z, c], own_sem.at[x])
            for x in range(2)
        ]
        for copy in own:
            copy.start()
        loads = [
            pltpu.make_async_copy(q_hbm, q, load_sem.at[0]),
            pltpu.make_async_copy(kv_hbm, kv, load_sem.at[1]),
            pltpu.make_async_copy(do_hbm, do, load_sem.at[2]),
            pltpu.make_async_copy(pq_hbm, pq_ref, load_sem.at[3]),
            pltpu.make_async_copy(qo_hbm, qo_ref, load_sem.at[4]),
        ]
        for copy in loads:
            copy.start()

        for copy in own:
            copy.wait()
        pl.semaphore_wait(barrier, n)

        gathers = {}
        forwards = {}

        def send_stored(x):
            for d in range(1, n):
                gathers[x, d] = pltpu.make_async_remote_copy(
                    src_ref=pre[x].at[z, c], dst_ref=pre[x].at[z, c],
                    send_sem=zs_sem.at[x, d], recv_sem=zr_sem.at[x, d],
                    device_id={"dp": lax.rem(z + d, n)},
                )
                gathers[x, d].start()
            forwards[x, 0] = pltpu.make_async_remote_copy(
                src_ref=pre[x].at[z, c], dst_ref=pre[x].at[z, c],
                send_sem=fs_sem.at[x, 0], recv_sem=fr_sem.at[x, 0], device_id={"seq": other},
            )
            forwards[x, 0].start()

        def forward_arrived(x):
            for d in range(1, n):
                gathers[x, d].wait_recv()
                source = lax.rem(z + n - d, n)
                forwards[x, d] = pltpu.make_async_remote_copy(
                    src_ref=pre[x].at[source, c], dst_ref=pre[x].at[source, c],
                    send_sem=fs_sem.at[x, d], recv_sem=fr_sem.at[x, d],
                    device_id={"seq": other},
                )
                forwards[x, d].start()

        def pick_prefix(x):
            for d in range(n):
                forwards[x, d].wait_recv()
            for p in range(count):
                rows = pre[x][slots[p]].reshape(prefix, HD)
                kv_pre[x, p] = rows
                kv_pre_t[x, p] = rows.T

        pairs = {}
        spreads = {}

        def half_term(x, d, half):
            slot = lax.rem(z + d, n)
            rows = pl.ds(pl.multiple_of(half * part, part), part)
            value = None
            for p in range(count):
                use = jnp.where(slots[p] == slot, SCALE if x == 0 else 1.0, 0.0).astype(F32)
                term = grad[p, x, rows, :] * use
                value = term if value is None else value + term
            return value

        def send_pairs(x):
            for d in list(range(1, n)) + [0]:
                send1[x, d] = half_term(x, d, other).astype(BF)
                pairs[x, d] = pltpu.make_async_remote_copy(
                    src_ref=send1.at[x, d], dst_ref=recv1.at[x, d],
                    send_sem=s1_sem.at[x, d], recv_sem=r1_sem.at[x, d],
                    device_id={"seq": other},
                )
                pairs[x, d].start()

        def send_spreads(x):
            for d in range(1, n):
                value = half_term(x, d, c)
                pairs[x, d].wait_recv()
                send2[x, d] = (value + recv1[x, d].astype(F32)).astype(BF)
                spreads[x, d] = pltpu.make_async_remote_copy(
                    src_ref=send2.at[x, d], dst_ref=recv2.at[x, d],
                    send_sem=s2_sem.at[x, d], recv_sem=r2_sem.at[x, d],
                    device_id={"dp": lax.rem(z + d, n)},
                )
                spreads[x, d].start()

        def finish(x):
            total = half_term(x, 0, c)
            pairs[x, 0].wait_recv()
            total = total + recv1[x, 0].astype(F32)
            for d in range(1, n):
                spreads[x, d].wait_recv()
                total = total + recv2[x, d].astype(F32)
            dpre[x, 0] = total.astype(BF)

        send_stored(0)
        for copy in loads:
            copy.wait()
        first = (z * 2 + c) * count
        slots = [qo_ref[pq_ref[first + p]] for p in range(count)]

        for p in range(count):
            kv_t[0, p] = kv[0, p].T
            kv_t[1, p] = kv[1, p].T
        key_at = lax.broadcasted_iota(jnp.int32, (tokens, tokens), 0)
        token_at = lax.broadcasted_iota(jnp.int32, (tokens, tokens), 1)

        def over_heads(step):
            def body(h, carry):
                for p in range(count):
                    step(p, h, pl.ds(pl.multiple_of(h * HD, HD), HD))
                return carry

            lax.fori_loop(0, heads, body, 0, unroll=UNROLL)

        def own_scores(p, h, cols):
            qt = q[p, :, cols].T
            q_t[p, h] = qt
            scores = jnp.where(key_at <= token_at, dot(kv[0, p], qt), MASKED)
            top = jnp.max(scores, axis=0, keepdims=True)
            e = jnp.exp2((scores - top) * EXP_SCALE)
            stat[p, h, 0:1, :] = top
            stat[p, h, 1:2, :] = jnp.sum(e, axis=0, keepdims=True)
            e_own[p, h] = e

        def own_values(p, h, cols):
            dt = do[p, :, cols].T
            do_t[p, h] = dt
            o_own[p, h] = dot(kv_t[1, p], e_own[p, h].astype(BF))
            dp_own[p, h] = dot(kv[1, p], dt)

        def prefix_scores(p, h, cols):
            scores = dot(kv_pre[0, p], q_t[p, h])
            top_own = stat[p, h, 0:1, :]
            top = jnp.maximum(top_own, jnp.max(scores, axis=0, keepdims=True))
            shrink = jnp.exp2((top_own - top) * EXP_SCALE)
            e = jnp.exp2((scores - top) * EXP_SCALE)
            total = stat[p, h, 1:2, :] * shrink + jnp.sum(e, axis=0, keepdims=True)
            inverse = 1.0 / total
            w = e * inverse
            w_pre[p, h] = w
            stat[p, h, 2:3, :] = shrink * inverse
            grad[p, 1] += dot(w.astype(BF), do[p, :, cols])

        def own_value_grad(p, h, cols):
            w = e_own[p, h] * stat[p, h, 2:3, :]
            own_grad[p, 1] += dot(w.astype(BF), do[p, :, cols])

        def prefix_values(p, h, cols):
            dt = do_t[p, h]
            w = w_pre[p, h]
            o = o_own[p, h] * stat[p, h, 2:3, :] + dot(kv_pre_t[1, p], w.astype(BF))
            o = o.astype(BF)
            o_t[p, h] = o
            delta = jnp.sum(dt.astype(F32) * o.astype(F32), axis=0, keepdims=True)
            stat[p, h, 3:4, :] = delta
            ds = (w * (dot(kv_pre[1, p], dt) - delta)).astype(BF)
            ds_pre[p, h] = ds
            grad[p, 0] += dot(ds, q[p, :, cols])

        def own_rest(p, h, cols):
            w = e_own[p, h] * stat[p, h, 2:3, :]
            ds = (w * (dp_own[p, h] - stat[p, h, 3:4, :])).astype(BF)
            own_grad[p, 0] += dot(ds, q[p, :, cols])
            back = dot(kv_t[0, p], ds) + dot(kv_pre_t[0, p], ds_pre[p, h])
            dq[p, :, cols] = (back * SCALE).astype(BF).T

        grad[...] = jnp.zeros_like(grad)
        own_grad[...] = jnp.zeros_like(own_grad)
        send_stored(1)
        over_heads(own_scores)
        forward_arrived(0)
        over_heads(own_values)
        pick_prefix(0)
        over_heads(prefix_scores)
        send_pairs(1)
        forward_arrived(1)
        over_heads(own_value_grad)
        send_spreads(1)
        pick_prefix(1)
        over_heads(prefix_values)
        send_pairs(0)
        for p in range(count):
            for h in range(heads):
                out[p, :, h * HD:(h + 1) * HD] = o_t[p, h].T
        store_out = pltpu.make_async_copy(out, out_hbm, store_sem.at[0])
        store_out.start()
        send_spreads(0)
        over_heads(own_rest)
        store_dq = pltpu.make_async_copy(dq, dq_hbm, store_sem.at[1])
        store_dq.start()
        for p in range(count):
            dkv[0, p] = (own_grad[p, 0] * SCALE).astype(BF)
            dkv[1, p] = own_grad[p, 1].astype(BF)
        store_dkv = pltpu.make_async_copy(dkv, dkv_hbm, store_sem.at[2])
        store_dkv.start()
        finish(1)
        finish(0)
        store_dpre = pltpu.make_async_copy(dpre, dpre_hbm, store_sem.at[3])
        store_dpre.start()

        for x in range(2):
            for d in range(n):
                if d:
                    gathers[x, d].wait_send()
                    spreads[x, d].wait_send()
                forwards[x, d].wait_send()
                pairs[x, d].wait_send()
        store_out.wait()
        store_dq.wait()
        store_dkv.wait()
        store_dpre.wait()

    return kernel

def store_kernel(*refs):
    sems = refs[-1]
    count = (len(refs) - 1) // 2
    copies = [
        pltpu.make_async_copy(refs[i], refs[count + i], sems.at[i]) for i in range(count)
    ]
    for copy in copies:
        copy.start()
    for copy in copies:
        copy.wait()


def store_all(arrays):
    any_spec = pl.BlockSpec(memory_space=pl.ANY)
    return pl.pallas_call(
        store_kernel,
        out_shape=tuple(jax.ShapeDtypeStruct(a.shape, a.dtype) for a in arrays),
        in_specs=[any_spec] * len(arrays),
        out_specs=(any_spec,) * len(arrays),
        scratch_shapes=[pltpu.SemaphoreType.DMA((len(arrays),))],
    )(*(pltpu.with_memory_space_constraint(a, pltpu.VMEM) for a in arrays))


def on_device(n, pas_q, pas_kv, pre_kv, d_out, passage_query, query_owner):
    count, tokens, width = pas_q.shape
    heads = width // HD
    part = pre_kv.shape[2]
    prefix = 2 * part
    assert pre_kv.shape[1] == 1
    any_spec = pl.BlockSpec(memory_space=pltpu.HBM)
    square = (count, heads, tokens, tokens)
    dma = pltpu.SemaphoreType.DMA
    call = pl.pallas_call(
        make_kernel(n, count, heads, tokens, part),
        out_shape=(
            jax.ShapeDtypeStruct(pas_q.shape, BF),
            jax.ShapeDtypeStruct(pas_q.shape, BF),
            jax.ShapeDtypeStruct(pas_kv.shape, BF),
            jax.ShapeDtypeStruct(pre_kv.shape, BF),
        ),
        in_specs=[any_spec] * 6,
        out_specs=(any_spec,) * 4,
        scratch_shapes=[
            pltpu.VMEM(pas_q.shape, BF),
            pltpu.VMEM(pas_q.shape, BF),
            pltpu.VMEM(pas_kv.shape, BF),
            pltpu.VMEM((count, heads, HD, tokens), BF),
            pltpu.VMEM((count, heads, HD, tokens), BF),
            pltpu.VMEM((2, count, HD, tokens), BF),
            pltpu.VMEM(square, F32),
            pltpu.VMEM(square, F32),
            pltpu.VMEM((count, heads, HD, tokens), F32),
            pltpu.VMEM((count, heads, prefix, tokens), BF),
            pltpu.VMEM((count, heads, HD, tokens), BF),
            pltpu.VMEM((count, heads, 8, tokens), F32),
            pltpu.VMEM((n, 2, part, HD), BF),
            pltpu.VMEM((n, 2, part, HD), BF),
            pltpu.VMEM((2, count, prefix, HD), BF),
            pltpu.VMEM((2, count, HD, prefix), BF),
            pltpu.VMEM((count, 2, prefix, HD), F32),
            pltpu.VMEM((count, 2, tokens, HD), F32),
            pltpu.VMEM((count, heads, prefix, tokens), F32),
            pltpu.VMEM(pas_q.shape, BF),
            pltpu.VMEM(pas_q.shape, BF),
            pltpu.VMEM(pas_kv.shape, BF),
            pltpu.VMEM(pre_kv.shape, BF),
            pltpu.VMEM((2, n, part, HD), BF),
            pltpu.VMEM((2, n, part, HD), BF),
            pltpu.VMEM((2, n, part, HD), BF),
            pltpu.VMEM((2, n, part, HD), BF),
            pltpu.SMEM(passage_query.shape, jnp.int32),
            pltpu.SMEM(query_owner.shape, jnp.int32),
            dma((5,)),
            dma((4,)),
            dma((2,)),
        ] + [dma((2, n))] * 8,
        compiler_params=pltpu.CompilerParams(
            collective_id=0, has_side_effects=True, vmem_limit_bytes=40 * 1024 * 1024
        ),
    )
    arrays = (passage_query, query_owner, pas_q, pas_kv, pre_kv, d_out)
    return store_all(call(*(pltpu.with_memory_space_constraint(a, pltpu.HBM) for a in arrays)))


def solution(mesh):
    n = mesh.shape["dp"]

    def step(*arrays):
        return on_device(n, *arrays)

    return jax.shard_map(
        step,
        mesh=mesh,
        in_specs=(
            P(("groups", "dp", "seq"), None, "tensor"),
            P(None, ("groups", "dp", "seq"), None, "tensor"),
            P(None, ("groups", "dp"), "seq", "tensor"),
            P(("groups", "dp", "seq"), None, "tensor"),
            P("groups"),
            P("groups"),
        ),
        out_specs=(
            P(("groups", "dp", "seq"), None, "tensor"),
            P(("groups", "dp", "seq"), None, "tensor"),
            P(None, ("groups", "dp", "seq"), None, "tensor"),
            P(None, ("groups", "dp"), "seq", "tensor"),
        ),
        check_vma=False,
    )
```

time: 26.7 us -> 23.3 us (0.87)
  Pallas kernels: 25.9 us -> 22.5 us
    pallas_call x1, Pallas kernels: 24.8 us -> 21.4 us  [on_device(): call(*(pltpu.with_memory_space_constraint(a, pltpu.HBM) for a in arrays))]
where the time goes in v3:
time: 23.3 us; the launch traced here: 23.2 us
  Pallas kernels  22.5 us (97%)
  between operations  0.64 us (3%)
    pallas_call x1, Pallas kernels, on_device(): call(*(pltpu.with_memory_space_constraint(a, pltpu.HBM) for a in arrays))  21.4 us
    pallas_call x1, Pallas kernels, store_all(): pl.pallas_call(store_kernel, out_shape=tuple((jax.ShapeDtypeStruct(a.shap...  1.1 us

profile of v3, /device:TPU:0, one launch (start us, length us, event | category | flops | bytes accessed | tf_op | source)
XLA Modules:
  0.0 23.2 jit_solution(9994057579343894190)
XLA Ops:
  0.6 21.4 %shard_map.93 = (bf16[2,256,512]{2,1,0:T(8,128)(2,1)S(1)}, bf16[2,256,512]{2,1,0:T(8,128)(2,1)S(1)}, bf16[2,2,256,128]{3,2,1,0:T(8,128)(2,1)S(1)}, bf16[2,1,128,128]{3,2,1,0:T(8,128)(2,1)S(1)}) custom-call(s32[16]{0:T(128)} %pq_hbm.1, s32[4]{0:T(128)} %qo_hbm.1, bf16[2,256,512]{2,1,0:T(8,128)(2,1)} %q_hbm.1, bf16[2,2,256,128]{3,2,1,0:T(8,128)(2,1)} %kv_hbm.1, ...), custom_call_target="tpu_custom_call" | custom-call | tf_op jit(solution)/shard_map/pallas_call | solution.py:346
  22.1 1.1 %shard_map.94 = (bf16[2,256,512]{2,1,0:T(8,128)(2,1)}, bf16[2,256,512]{2,1,0:T(8,128)(2,1)}, bf16[2,2,256,128]{3,2,1,0:T(8,128)(2,1)}, bf16[2,1,128,128]{3,2,1,0:T(8,128)(2,1)}) custom-call(bf16[2,256,512]{2,1,0:T(8,128)(2,1)S(1)} %get-tuple-element.8.refs_0_, bf16[2,256,512]{2,1,0:T(8,128)(2,1)S(1)} %get-tuple-element.9.refs_1_, ...), custom_call_target="tpu_custom_call" | custom-call | tf_op jit(solution)/shard_map/pallas_call | solution.py:279

commit v4 on v3

--- a/solution.py
+++ b/solution.py
@@ -13,7 +13,6 @@
 MASKED = -1e30
 BF = jnp.bfloat16
 F32 = jnp.float32
-UNROLL = 4
 
 
 def dot(a, b):
@@ -22,14 +21,15 @@
 
 def make_kernel(n, count, heads, tokens, part):
     prefix = 2 * part
+    order = list(range(1, n))
 
     def kernel(
         pq_hbm, qo_hbm, q_hbm, kv_hbm, pre_hbm, do_hbm,
-        out_hbm, dq_hbm, dkv_hbm, dpre_hbm,
+        out, dq, dkv, dpre,
         q, do, kv, q_t, do_t, kv_t, e_own, dp_own, o_own, ds_pre, o_t, stat,
-        pre_k, pre_v, kv_pre, kv_pre_t, grad, own_grad, w_pre, out, dq, dkv, dpre,
+        pre_k, pre_v, kv_pre, kv_pre_t, grad, own_grad, total, w_pre,
         send1, recv1, send2, recv2,
-        pq_ref, qo_ref, load_sem, store_sem, own_sem,
+        pq_ref, qo_ref, load_sem, own_sem,
         zs_sem, zr_sem, fs_sem, fr_sem, s1_sem, r1_sem, s2_sem, r2_sem,
     ):
         z = lax.axis_index("dp")
@@ -66,7 +66,7 @@
         forwards = {}
 
         def send_stored(x):
-            for d in range(1, n):
+            for d in order:
                 gathers[x, d] = pltpu.make_async_remote_copy(
                     src_ref=pre[x].at[z, c], dst_ref=pre[x].at[z, c],
                     send_sem=zs_sem.at[x, d], recv_sem=zr_sem.at[x, d],
@@ -80,7 +80,7 @@
             forwards[x, 0].start()
 
         def forward_arrived(x):
-            for d in range(1, n):
+            for d in order:
                 gathers[x, d].wait_recv()
                 source = lax.rem(z + n - d, n)
                 forwards[x, d] = pltpu.make_async_remote_copy(
@@ -101,52 +101,56 @@
         pairs = {}
         spreads = {}
 
-        def half_term(x, d, half):
+        def half_term(x, d):
             slot = lax.rem(z + d, n)
-            rows = pl.ds(pl.multiple_of(half * part, part), part)
+            rows = pl.ds(pl.multiple_of(c * part, part), part)
             value = None
             for p in range(count):
-                use = jnp.where(slots[p] == slot, SCALE if x == 0 else 1.0, 0.0).astype(F32)
-                term = grad[p, x, rows, :] * use
+                scale = SCALE if x == 0 else 1.0
+                use = jnp.where(slots[p] == slot, scale, 0.0).astype(F32)
+                use_far = jnp.where(far_slots[p] == slot, 1.0, 0.0).astype(F32)
+                term = grad[p, x, rows, :] * use + recv1[x, p].astype(F32) * use_far
                 value = term if value is None else value + term
             return value
 
-        def send_pairs(x):
-            for d in list(range(1, n)) + [0]:
-                send1[x, d] = half_term(x, d, other).astype(BF)
-                pairs[x, d] = pltpu.make_async_remote_copy(
-                    src_ref=send1.at[x, d], dst_ref=recv1.at[x, d],
-                    send_sem=s1_sem.at[x, d], recv_sem=r1_sem.at[x, d],
-                    device_id={"seq": other},
-                )
-                pairs[x, d].start()
+        def send_pair(x, p):
+            rows = pl.ds(pl.multiple_of(other * part, part), part)
+            term = grad[p, x, rows, :]
+            send1[x, p] = (term * SCALE if x == 0 else term).astype(BF)
+            pairs[x, p] = pltpu.make_async_remote_copy(
+                src_ref=send1.at[x, p], dst_ref=recv1.at[x, p],
+                send_sem=s1_sem.at[x, p], recv_sem=r1_sem.at[x, p],
+                device_id={"seq": other},
+            )
+            pairs[x, p].start()
 
         def send_spreads(x):
-            for d in range(1, n):
-                value = half_term(x, d, c)
-                pairs[x, d].wait_recv()
-                send2[x, d] = (value + recv1[x, d].astype(F32)).astype(BF)
+            for p in range(count):
+                pairs[x, p].wait_recv()
+            for d in order:
+                send2[x, d] = half_term(x, d).astype(BF)
                 spreads[x, d] = pltpu.make_async_remote_copy(
                     src_ref=send2.at[x, d], dst_ref=recv2.at[x, d],
                     send_sem=s2_sem.at[x, d], recv_sem=r2_sem.at[x, d],
                     device_id={"dp": lax.rem(z + d, n)},
                 )
                 spreads[x, d].start()
+            total[x] = half_term(x, 0)
 
         def finish(x):
-            total = half_term(x, 0, c)
-            pairs[x, 0].wait_recv()
-            total = total + recv1[x, 0].astype(F32)
-            for d in range(1, n):
+            value = total[x]
+            for d in order:
                 spreads[x, d].wait_recv()
-                total = total + recv2[x, d].astype(F32)
-            dpre[x, 0] = total.astype(BF)
+                value = value + recv2[x, d].astype(F32)
+            dpre[x, 0] = value.astype(BF)
 
         send_stored(0)
         for copy in loads:
             copy.wait()
         first = (z * 2 + c) * count
         slots = [qo_ref[pq_ref[first + p]] for p in range(count)]
+        first_far = (z * 2 + other) * count
+        far_slots = [qo_ref[pq_ref[first_far + p]] for p in range(count)]
 
         for p in range(count):
             kv_t[0, p] = kv[0, p].T
@@ -154,13 +158,14 @@
         key_at = lax.broadcasted_iota(jnp.int32, (tokens, tokens), 0)
         token_at = lax.broadcasted_iota(jnp.int32, (tokens, tokens), 1)
 
+        def passage(step, p):
+            for h in range(heads):
+                step(p, h, slice(h * HD, (h + 1) * HD))
+
         def over_heads(step):
-            def body(h, carry):
+            for h in range(heads):
                 for p in range(count):
-                    step(p, h, pl.ds(pl.multiple_of(h * HD, HD), HD))
-                return carry
-
-            lax.fori_loop(0, heads, body, 0, unroll=UNROLL)
+                    step(p, h, slice(h * HD, (h + 1) * HD))
 
         def own_scores(p, h, cols):
             qt = q[p, :, cols].T
@@ -184,8 +189,8 @@
             top = jnp.maximum(top_own, jnp.max(scores, axis=0, keepdims=True))
             shrink = jnp.exp2((top_own - top) * EXP_SCALE)
             e = jnp.exp2((scores - top) * EXP_SCALE)
-            total = stat[p, h, 1:2, :] * shrink + jnp.sum(e, axis=0, keepdims=True)
-            inverse = 1.0 / total
+            norm = stat[p, h, 1:2, :] * shrink + jnp.sum(e, axis=0, keepdims=True)
+            inverse = 1.0 / norm
             w = e * inverse
             w_pre[p, h] = w
             stat[p, h, 2:3, :] = shrink * inverse
@@ -222,31 +227,25 @@
         over_heads(own_values)
         pick_prefix(0)
         over_heads(prefix_scores)
-        send_pairs(1)
+        for p in range(count):
+            send_pair(1, p)
         forward_arrived(1)
         over_heads(own_value_grad)
         send_spreads(1)
         pick_prefix(1)
         over_heads(prefix_values)
-        send_pairs(0)
+        for p in range(count):
+            send_pair(0, p)
         for p in range(count):
             for h in range(heads):
                 out[p, :, h * HD:(h + 1) * HD] = o_t[p, h].T
-        store_out = pltpu.make_async_copy(out, out_hbm, store_sem.at[0])
-        store_out.start()
         send_spreads(0)
         over_heads(own_rest)
-        store_dq = pltpu.make_async_copy(dq, dq_hbm, store_sem.at[1])
-        store_dq.start()
         for p in range(count):
             dkv[0, p] = (own_grad[p, 0] * SCALE).astype(BF)
             dkv[1, p] = own_grad[p, 1].astype(BF)
-        store_dkv = pltpu.make_async_copy(dkv, dkv_hbm, store_sem.at[2])
-        store_dkv.start()
         finish(1)
         finish(0)
-        store_dpre = pltpu.make_async_copy(dpre, dpre_hbm, store_sem.at[3])
-        store_dpre.start()
 
         for x in range(2):
             for d in range(n):
@@ -254,11 +253,8 @@
                     gathers[x, d].wait_send()
                     spreads[x, d].wait_send()
                 forwards[x, d].wait_send()
-                pairs[x, d].wait_send()
-        store_out.wait()
-        store_dq.wait()
-        store_dkv.wait()
-        store_dpre.wait()
+            for p in range(count):
+                pairs[x, p].wait_send()
 
     return kernel
 
@@ -303,7 +299,7 @@
             jax.ShapeDtypeStruct(pre_kv.shape, BF),
         ),
         in_specs=[any_spec] * 6,
-        out_specs=(any_spec,) * 4,
+        out_specs=(pl.BlockSpec(memory_space=pltpu.VMEM),) * 4,
         scratch_shapes=[
             pltpu.VMEM(pas_q.shape, BF),
             pltpu.VMEM(pas_q.shape, BF),
@@ -323,21 +319,17 @@
             pltpu.VMEM((2, count, HD, prefix), BF),
             pltpu.VMEM((count, 2, prefix, HD), F32),
             pltpu.VMEM((count, 2, tokens, HD), F32),
+            pltpu.VMEM((2, part, HD), F32),
             pltpu.VMEM((count, heads, prefix, tokens), F32),
-            pltpu.VMEM(pas_q.shape, BF),
-            pltpu.VMEM(pas_q.shape, BF),
-            pltpu.VMEM(pas_kv.shape, BF),
-            pltpu.VMEM(pre_kv.shape, BF),
-            pltpu.VMEM((2, n, part, HD), BF),
-            pltpu.VMEM((2, n, part, HD), BF),
+            pltpu.VMEM((2, count, part, HD), BF),
+            pltpu.VMEM((2, count, part, HD), BF),
             pltpu.VMEM((2, n, part, HD), BF),
             pltpu.VMEM((2, n, part, HD), BF),
             pltpu.SMEM(passage_query.shape, jnp.int32),
             pltpu.SMEM(query_owner.shape, jnp.int32),
             dma((5,)),
-            dma((4,)),
             dma((2,)),
-        ] + [dma((2, n))] * 8,
+        ] + [dma((2, n))] * 4 + [dma((2, count))] * 2 + [dma((2, n))] * 2,
         compiler_params=pltpu.CompilerParams(
             collective_id=0, has_side_effects=True, vmem_limit_bytes=40 * 1024 * 1024
         ),

time: 23.3 us -> 23 us (0.987)
  Pallas kernels: 22.5 us -> 22.2 us
    pallas_call x1, Pallas kernels: 21.4 us -> 21.1 us  [on_device(): call(*(pltpu.with_memory_space_constraint(a, pltpu.HBM) for a in arrays))]
where the time goes in v4:
time: 23 us; the launch traced here: 22.9 us
  Pallas kernels  22.2 us (97%)
  between operations  0.64 us (3%)
    pallas_call x1, Pallas kernels, on_device(): call(*(pltpu.with_memory_space_constraint(a, pltpu.HBM) for a in arrays))  21.1 us
    pallas_call x1, Pallas kernels, store_all(): pl.pallas_call(store_kernel, out_shape=tuple((jax.ShapeDtypeStruct(a.shap...  1.1 us

profile of v4, /device:TPU:0, one launch (start us, length us, event | category | flops | bytes accessed | tf_op | source)
XLA Modules:
  0.0 22.9 jit_solution(8496141102495696312)
XLA Ops:
  0.6 21.1 %shard_map.93 = (bf16[2,256,512]{2,1,0:T(8,128)(2,1)S(1)}, bf16[2,256,512]{2,1,0:T(8,128)(2,1)S(1)}, bf16[2,2,256,128]{3,2,1,0:T(8,128)(2,1)S(1)}, bf16[2,1,128,128]{3,2,1,0:T(8,128)(2,1)S(1)}) custom-call(s32[16]{0:T(128)} %pq_hbm.1, s32[4]{0:T(128)} %qo_hbm.1, bf16[2,256,512]{2,1,0:T(8,128)(2,1)} %q_hbm.1, bf16[2,2,256,128]{3,2,1,0:T(8,128)(2,1)} %kv_hbm.1, ...), custom_call_target="tpu_custom_call" | custom-call | tf_op jit(solution)/shard_map/pallas_call | solution.py:338
  21.8 1.1 %shard_map.94 = (bf16[2,256,512]{2,1,0:T(8,128)(2,1)}, bf16[2,256,512]{2,1,0:T(8,128)(2,1)}, bf16[2,2,256,128]{3,2,1,0:T(8,128)(2,1)}, bf16[2,1,128,128]{3,2,1,0:T(8,128)(2,1)}) custom-call(bf16[2,256,512]{2,1,0:T(8,128)(2,1)S(1)} %get-tuple-element.8.refs_0_, bf16[2,256,512]{2,1,0:T(8,128)(2,1)S(1)} %get-tuple-element.9.refs_1_, ...), custom_call_target="tpu_custom_call" | custom-call | tf_op jit(solution)/shard_map/pallas_call | solution.py:275

commit v5 on v4

--- a/solution.py
+++ b/solution.py
@@ -27,7 +27,7 @@
         pq_hbm, qo_hbm, q_hbm, kv_hbm, pre_hbm, do_hbm,
         out, dq, dkv, dpre,
         q, do, kv, q_t, do_t, kv_t, e_own, dp_own, o_own, ds_pre, o_t, stat,
-        pre_k, pre_v, kv_pre, kv_pre_t, grad, own_grad, total, w_pre,
+        pre_k, pre_v, kv_pre, kv_pre_t, grad, own_grad, total, near, w_pre,
         send1, recv1, send2, recv2,
         pq_ref, qo_ref, load_sem, own_sem,
         zs_sem, zr_sem, fs_sem, fr_sem, s1_sem, r1_sem, s2_sem, r2_sem,
@@ -101,17 +101,16 @@
         pairs = {}
         spreads = {}
 
-        def half_term(x, d):
-            slot = lax.rem(z + d, n)
+        def use(at, p, d):
+            return jnp.where(at[p] == lax.rem(z + d, n), 1.0, 0.0).astype(F32)
+
+        def near_term(x, d):
             rows = pl.ds(pl.multiple_of(c * part, part), part)
-            value = None
-            for p in range(count):
-                scale = SCALE if x == 0 else 1.0
-                use = jnp.where(slots[p] == slot, scale, 0.0).astype(F32)
-                use_far = jnp.where(far_slots[p] == slot, 1.0, 0.0).astype(F32)
-                term = grad[p, x, rows, :] * use + recv1[x, p].astype(F32) * use_far
-                value = term if value is None else value + term
-            return value
+            scale = SCALE if x == 0 else 1.0
+            return sum(grad[p, x, rows, :] * (use(slots, p, d) * scale) for p in range(count))
+
+        def far_term(x, d):
+            return sum(recv1[x, p].astype(F32) * use(far_slots, p, d) for p in range(count))
 
         def send_pair(x, p):
             rows = pl.ds(pl.multiple_of(other * part, part), part)
@@ -125,17 +124,19 @@
             pairs[x, p].start()
 
         def send_spreads(x):
+            for d in range(n):
+                near[d] = near_term(x, d)
             for p in range(count):
                 pairs[x, p].wait_recv()
             for d in order:
-                send2[x, d] = half_term(x, d).astype(BF)
+                send2[x, d] = (near[d] + far_term(x, d)).astype(BF)
                 spreads[x, d] = pltpu.make_async_remote_copy(
                     src_ref=send2.at[x, d], dst_ref=recv2.at[x, d],
                     send_sem=s2_sem.at[x, d], recv_sem=r2_sem.at[x, d],
                     device_id={"dp": lax.rem(z + d, n)},
                 )
                 spreads[x, d].start()
-            total[x] = half_term(x, 0)
+            total[x] = near[0] + far_term(x, 0)
 
         def finish(x):
             value = total[x]
@@ -320,6 +321,7 @@
             pltpu.VMEM((count, 2, prefix, HD), F32),
             pltpu.VMEM((count, 2, tokens, HD), F32),
             pltpu.VMEM((2, part, HD), F32),
+            pltpu.VMEM((n, part, HD), F32),
             pltpu.VMEM((count, heads, prefix, tokens), F32),
             pltpu.VMEM((2, count, part, HD), BF),
             pltpu.VMEM((2, count, part, HD), BF),

time: 23 us -> 23 us (level)
  no operation moved by 1% of the time
where the time goes in v5:
time: 23 us; the launch traced here: 22.9 us
  Pallas kernels  22.2 us (97%)
  between operations  0.64 us (3%)
    pallas_call x1, Pallas kernels, on_device(): call(*(pltpu.with_memory_space_constraint(a, pltpu.HBM) for a in arrays))  21.1 us
    pallas_call x1, Pallas kernels, store_all(): pl.pallas_call(store_kernel, out_shape=tuple((jax.ShapeDtypeStruct(a.shap...  1.1 us

profile of v5, /device:TPU:0, one launch (start us, length us, event | category | flops | bytes accessed | tf_op | source)
XLA Modules:
  0.0 22.9 jit_solution(8470064984591680452)
XLA Ops:
  0.6 21.1 %shard_map.93 = (bf16[2,256,512]{2,1,0:T(8,128)(2,1)S(1)}, bf16[2,256,512]{2,1,0:T(8,128)(2,1)S(1)}, bf16[2,2,256,128]{3,2,1,0:T(8,128)(2,1)S(1)}, bf16[2,1,128,128]{3,2,1,0:T(8,128)(2,1)S(1)}) custom-call(s32[16]{0:T(128)} %pq_hbm.1, s32[4]{0:T(128)} %qo_hbm.1, bf16[2,256,512]{2,1,0:T(8,128)(2,1)} %q_hbm.1, bf16[2,2,256,128]{3,2,1,0:T(8,128)(2,1)} %kv_hbm.1, ...), custom_call_target="tpu_custom_call" | custom-call | tf_op jit(solution)/shard_map/pallas_call | solution.py:340
  21.8 1.1 %shard_map.94 = (bf16[2,256,512]{2,1,0:T(8,128)(2,1)}, bf16[2,256,512]{2,1,0:T(8,128)(2,1)}, bf16[2,2,256,128]{3,2,1,0:T(8,128)(2,1)}, bf16[2,1,128,128]{3,2,1,0:T(8,128)(2,1)}) custom-call(bf16[2,256,512]{2,1,0:T(8,128)(2,1)S(1)} %get-tuple-element.8.refs_0_, bf16[2,256,512]{2,1,0:T(8,128)(2,1)S(1)} %get-tuple-element.9.refs_1_, ...), custom_call_target="tpu_custom_call" | custom-call | tf_op jit(solution)/shard_map/pallas_call | solution.py:276
